TPU v7x, 32 devices: a whole 2x2x4 slice. The times are simulated.
32 devices in a mesh: gx: 4 (over y, x), gy: 4 (over z), gz: 2 (over core).
Axes of the slice: x: 2, y: 2, z: 4, core: 2. Of those that a mesh axis runs over, the one named last changes fastest.
Arguments:
- boxes: bfloat16 [4, 4, 2, 16, 16, 256], P('gx', 'gy', 'gz'), may hold values from 0 to 2
- anchors: int32 [4, 4, 2, 16, 3], P('gx', 'gy', 'gz'), may hold values from 0 to 4, as said below
- potential: float32 [160, 160, 80], P('gx', 'gy', 'gz'), may hold values from 0.5 to 2
Outputs:
- relaxed: bfloat16 [4, 4, 2, 16, 16, 256], P('gx', 'gy', 'gz')
Inputs may be any that keep to these rules, and one draw needn't show every extreme that they name: `anchors`: in every region exactly 8 of the 16 functions are border functions, and every coordinate of theirs is 0 or 4; all coordinates of the others lie within 1 to 3.
All inputs are finite; a program needn't handle non-finite values.
Results may differ from a plain program's by a relative error of at most 0.0041.
Values may be sent and summed in bfloat16 or wider, within the bound.
A program may use at most 128 MiB of HBM per device.

v0:
```python
import jax
import jax.numpy as jnp
from jax import lax
from jax.sharding import PartitionSpec as P

EXPORT = 8
REGION = 5
SWEEPS = 2


MAGIC = [
    8.433424733352934e-07,
    -1.290557201342061e-05,
    8.76298447621056e-05,
    -0.00030158038132690465,
    0.001747237136729939,
    -0.009420470302010804,
    0.023738214637249424,
    0.0612625895831208,
    0.9940415697834004,
    -0.06048952891969835,
    -0.021030251609303816,
    0.013372634148547948,
    -0.0034412814449349387,
    0.0004944322768868992,
    -5.185986881173433e-05,
    2.7273449291197967e-06,
]
KINETIC = [
    -3.55369228991319,
    2.2191465938911166,
    -0.6156141465570069,
    0.2371780582153806,
    -0.0822663999742123,
    0.0220702918848226,
    -0.004097656893426338,
    0.00045167920287502236,
    -2.3982285245075998e-05,
    2.0904234952920368e-06,
    -3.7230763047369276e-07,
    -1.0585705549674146e-08,
    -5.8138798302825403e-11,
    2.7080049362631943e-13,
    -6.9244749406392e-18,
]
CELL = 1.0 / 4096.0
STEP = 0.1
PENALTY = 3.0


def passed_along(value, axis, steps):
    count = lax.axis_size(axis)
    pairs = [(source, (source + steps) % count) for source in range(count)]
    return lax.ppermute(value, axis, pairs)


def padded(block, sides, width):
    for axis, dim in sides:
        count = lax.axis_size(axis)
        forward = [(i, i + 1) for i in range(count - 1)]
        forward.append((count - 1, 0))
        backward = [(target, source) for source, target in forward]
        low = lax.ppermute(
            lax.slice_in_dim(block, block.shape[dim] - width, None, axis=dim), axis, forward
        )
        high = lax.ppermute(lax.slice_in_dim(block, 0, width, axis=dim), axis, backward)
        block = jnp.concatenate([low, block, high], axis=dim)
    return block


def magic_table(amount):
    row_ids = jnp.arange(amount)[:, None]
    col_ids = jnp.arange(amount)[None, :]
    offset = col_ids - row_ids + 8
    coeffs = jnp.array(MAGIC, dtype=jnp.float32)
    picked = coeffs[jnp.clip(offset, 0, 15)]
    return jnp.where((offset >= 0) & (offset < 16), picked, jnp.zeros_like(picked))


def kinetic_table(amount):
    row_ids = jnp.arange(amount)[:, None]
    col_ids = jnp.arange(amount)[None, :]
    distance = jnp.abs(col_ids - row_ids)
    coeffs = jnp.array(KINETIC, dtype=jnp.float32)
    picked = coeffs[jnp.clip(distance, 0, 14)]
    return jnp.where(distance < 15, picked, jnp.zeros_like(picked))


def apply_hamiltonian(values, potential_box):
    highest = lax.Precision.HIGHEST
    amount = values.shape[1]
    magic = magic_table(amount)
    second = kinetic_table(amount)
    identity_small = jnp.eye(amount, dtype=jnp.float32)
    magic_pair = jnp.kron(magic, magic)
    second_pair = jnp.kron(second, identity_small) + jnp.kron(identity_small, second)
    on_grid = jnp.einsum("xw,fwc->fxc", magic, values, precision=highest)
    on_grid = jnp.einsum("dc,fxc->fxd", magic_pair, on_grid, precision=highest)
    weighted = potential_box * on_grid
    returned = jnp.einsum("wx,fwc->fxc", magic, weighted, precision=highest)
    returned = jnp.einsum("cd,fxc->fxd", magic_pair, returned, precision=highest)
    kinetic = jnp.einsum("xw,fwc->fxc", second, values, precision=highest)
    kinetic = kinetic + jnp.einsum("dc,fxc->fxd", second_pair, values, precision=highest)
    return returned - 0.5 * kinetic


def border_rows(anchor_rows):
    amount = anchor_rows.shape[0]
    touching = jnp.any((anchor_rows == 0) | (anchor_rows == REGION - 1), axis=1).astype(jnp.int32)
    ranking = jnp.cumsum(touching) - touching
    places = jnp.arange(EXPORT, dtype=jnp.int32)
    matched = (touching[None, :] == 1) & (ranking[None, :] == places[:, None])
    numbers = jnp.arange(amount, dtype=jnp.int32)[None, :]
    return jnp.sum(jnp.where(matched, numbers, 0), axis=1)


def octants(values):
    amount = values.shape[0]
    half_width = values.shape[1] // 2
    split_up = values.reshape(amount, 2, half_width, 2, half_width, 2, half_width)
    return split_up.transpose(0, 1, 3, 5, 2, 4, 6).reshape(amount * 8, half_width**3)


def from_octants(values, amount, width):
    half_width = width // 2
    split_up = values.reshape(amount, 2, 2, 2, half_width, half_width, half_width)
    return split_up.transpose(0, 1, 4, 2, 5, 3, 6).reshape(amount, width, width * width)


def octant_mask(left_anchor, right_anchor):
    labels = jnp.arange(8, dtype=jnp.int32)
    corner_bits = jnp.stack([labels // 4, labels // 2 % 2, labels % 2], axis=1)
    left_place = left_anchor[:, None, :] + corner_bits[None]
    right_place = right_anchor[:, None, :] + corner_bits[None]
    result = jnp.ones((left_anchor.shape[0], 8, right_anchor.shape[0], 8), jnp.float32)
    for dimension in range(3):
        equal = left_place[:, :, None, None, dimension] == right_place[None, None, :, :, dimension]
        result = result * equal.astype(jnp.float32)
    return result


def combine(current, own_anchor, applied, cand_boxes, cand_anchor):
    func_count = current.shape[0]
    cand_count = cand_boxes.shape[0]
    width = current.shape[1]
    stacked = octants(jnp.concatenate([current, applied.astype(jnp.bfloat16)], axis=0))
    columns = octants(cand_boxes)
    products = jnp.einsum("ak,bk->ab", stacked, columns, preferred_element_type=jnp.float32)
    products = products.reshape(2, func_count, 8, cand_count, 8)
    geometry = octant_mask(own_anchor, cand_anchor)
    intersection = CELL * jnp.sum(products * geometry[None], axis=(2, 4))
    identity = (jnp.arange(func_count)[:, None] == jnp.arange(cand_count)[None, :]).astype(
        jnp.float32
    )
    coupling = intersection[1] - PENALTY * (intersection[0] - identity)
    weights = (
        (coupling[:, None, :, None] * geometry)
        .astype(jnp.bfloat16)
        .reshape(func_count * 8, cand_count * 8)
    )
    correction = jnp.dot(weights, columns, preferred_element_type=jnp.float32)
    correction = from_octants(correction, func_count, width)
    return (current.astype(jnp.float32) - STEP * (applied - correction)).astype(jnp.bfloat16)


def neighbour_offsets():
    labels = jnp.arange(27, dtype=jnp.int32)
    return jnp.stack([labels // 9 - 1, labels // 3 % 3 - 1, labels % 3 - 1], axis=1)


def local(boxes, anchors, potential):
    width = boxes.shape[4]
    half_width = width // 2
    func_count = boxes.shape[3]
    own_anchor = anchors[0, 0, 0]
    extended = potential
    upper_x = passed_along(extended[:half_width].astype(jnp.bfloat16), "gx", -1).astype(jnp.float32)
    extended = jnp.concatenate([extended, upper_x], axis=0)
    upper_y = passed_along(extended[:, :half_width].astype(jnp.bfloat16), "gy", -1).astype(
        jnp.float32
    )
    extended = jnp.concatenate([extended, upper_y], axis=1)
    upper_z = passed_along(extended[:, :, :half_width].astype(jnp.bfloat16), "gz", -1).astype(
        jnp.float32
    )
    extended = jnp.concatenate([extended, upper_z], axis=2)

    def cut_box(anchor_row):
        start = half_width * anchor_row
        return lax.dynamic_slice(extended, (start[0], start[1], start[2]), (width, width, width))

    potential_box = jax.vmap(cut_box)(own_anchor).reshape(func_count, width, width * width)
    shifted_by = REGION * neighbour_offsets()
    current = boxes[0, 0, 0]
    for sweep_index in range(SWEEPS):
        applied = apply_hamiltonian(current.astype(jnp.float32), potential_box)
        chosen = border_rows(own_anchor)
        leaving_boxes = current[chosen]
        leaving_anchor = own_anchor[chosen].astype(jnp.bfloat16)
        near_boxes, near_anchor = (
            padded(leaving_boxes[None, None, None], (("gx", 0), ("gy", 1), ("gz", 2)), 1),
            padded(leaving_anchor[None, None, None], (("gx", 0), ("gy", 1), ("gz", 2)), 1),
        )
        picked_boxes = near_boxes.reshape(27, EXPORT, width, width * width)
        picked_anchor = near_anchor.reshape(27, EXPORT, 3).astype(jnp.int32)
        placed_anchor = picked_anchor + shifted_by[:, None, :]
        cand_boxes = jnp.concatenate(
            [
                current,
                picked_boxes[:13].reshape(-1, width, width * width),
                picked_boxes[14:].reshape(-1, width, width * width),
            ],
            axis=0,
        )
        cand_anchor = jnp.concatenate(
            [own_anchor, placed_anchor[:13].reshape(-1, 3), placed_anchor[14:].reshape(-1, 3)],
            axis=0,
        )
        current = combine(current, own_anchor, applied, cand_boxes, cand_anchor)
    return current[None, None, None]


def solution(mesh):
    placed = (
        P("gx", "gy", "gz", None, None, None),
        P("gx", "gy", "gz", None, None),
        P("gx", "gy", "gz"),
    )
    return jax.shard_map(
        local,
        mesh=mesh,
        in_specs=placed,
        out_specs=P("gx", "gy", "gz", None, None, None),
        check_vma=False,
    )
```

profile of v0, /device:TPU:0, one launch (start us, length us, event | category | flops | bytes accessed | tf_op | source)
XLA Modules:
  0.0 544.0 jit_solution(8356232703443918478)
XLA Ops:
  2.5 3.9 collective-permute-start.10
  30.9 3.7 collective-permute-start.12
  35.8 4.1 collective-permute-done.11
  51.1 8.6 %collective-permute-done.1 = bf16[48,8,40]{1,2,0:T(8,128)(2,1)} collective-permute-done((bf16[48,8,40]{1,2,0:T(8,128)(2,1)}, bf16[48,8,40]{1,2,0:T(8,128)(2,1)}, u32[]{:S(2)}, u32[]{:S(2)}) %collective-permute-start.1) | collective-permute-done | bytes 30752 | tf_op jit(solution)/shard_map/ppermute | solution.py:54
  66.3 80.4 %while.1 = (s32[]{:T(128)}, f32[48,48,48]{1,2,0:T(8,128)}, s32[16,3]{0,1:T(4,128)}, f32[16,16,16,16]{3,2,1,0:T(8,128)}, s32[]{:T(128)}) while((s32[]{:T(128)}, f32[48,48,48]{1,2,0:T(8,128)}, s32[16,3]{0,1:T(4,128)}, f32[16,16,16,16]{3,2,1,0:T(8,128)}, s32[]{:T(128)}) %tuple.43), condition=%wide.while_cond, body=%wide.while_body.sunk | while | flops 2 | bytes 213121 | solution.py:190
  158.2 3.9 dot_general.73
  165.9 16.9 %concatenate.89 = bf16[104,2,8,2,8,2,8]{6,5,4,3,2,1,0:T(2,128)(2,1)} reshape(bf16[13,8,16,256]{3,2,1,0:T(8,128)(2,1)S(1)} %get-tuple-element.38) | data formatting | bytes 1703936 | tf_op jit(solution)/shard_map/concatenate | solution.py:207
  182.8 29.5 %copy.152 = bf16[104,2,8,2,8,2,8]{0,6,5,4,3,2,1:T(8,128)(2,1)} copy(bf16[104,2,8,2,8,2,8]{6,5,4,3,2,1,0:T(2,128)(2,1)} %concatenate.89) | data formatting | bytes 1703936 | tf_op jit(solution)/shard_map/concatenate | solution.py:207
  212.3 16.9 %concatenate.90 = bf16[104,2,8,2,8,2,8]{6,5,4,3,2,1,0:T(2,128)(2,1)} reshape(bf16[13,8,16,256]{3,2,1,0:T(8,128)(2,1)S(1)} %get-tuple-element.39) | data formatting | bytes 1703936 | tf_op jit(solution)/shard_map/concatenate | solution.py:207
  229.2 29.5 %copy.153 = bf16[104,2,8,2,8,2,8]{0,6,5,4,3,2,1:T(8,128)(2,1)} copy(bf16[104,2,8,2,8,2,8]{6,5,4,3,2,1,0:T(2,128)(2,1)} %concatenate.90) | data formatting | bytes 1703936 | tf_op jit(solution)/shard_map/concatenate | solution.py:207
  263.6 20.5 %copy.168 = bf16[224,2,2,2,8,8,8]{6,5,4,3,2,1,0:T(8,128)(2,1)} copy(bf16[224,2,2,2,8,8,8]{0,6,3,5,2,4,1:T(8,128)(2,1)S(1)} %maximum_bitcast_fusion) | data formatting | bytes 3670016 | tf_op jit(solution)/shard_map/transpose | solution.py:121
  287.0 42.2 %reshape.799 = bf16[1792,512]{1,0:T(8,128)(2,1)S(1)} reshape(bf16[224,2,2,2,8,8,8]{6,5,4,3,2,1,0:T(8,128)(2,1)} %copy.168) | data formatting | bytes 3670016 | tf_op jit(solution)/shard_map/reshape | solution.py:121
  331.9 3.6 convolution_bitcast_fusion.1
  344.6 3.8 collective-permute-start.18
  348.7 5.0 collective-permute-done.18
  353.8 3.5 collective-permute-done.17
  362.0 4.1 dot_general.85
  371.1 18.1 %concatenate.101 = bf16[104,2,8,2,8,2,8]{6,5,4,3,2,1,0:T(2,128)(2,1)} reshape(bf16[13,8,16,256]{3,2,1,0:T(8,128)(2,1)} %get-tuple-element.36) | data formatting | bytes 1703936 | tf_op jit(solution)/shard_map/concatenate | solution.py:207
  389.2 29.5 %copy.176 = bf16[104,2,8,2,8,2,8]{0,6,5,4,3,2,1:T(8,128)(2,1)} copy(bf16[104,2,8,2,8,2,8]{6,5,4,3,2,1,0:T(2,128)(2,1)} %concatenate.101) | data formatting | bytes 1703936 | tf_op jit(solution)/shard_map/concatenate | solution.py:207
  418.8 16.9 %concatenate.102 = bf16[104,2,8,2,8,2,8]{6,5,4,3,2,1,0:T(2,128)(2,1)} reshape(bf16[13,8,16,256]{3,2,1,0:T(8,128)(2,1)S(1)} %copy-done.4) | data formatting | bytes 1703936 | tf_op jit(solution)/shard_map/concatenate | solution.py:207
  435.7 29.5 %copy.177 = bf16[104,2,8,2,8,2,8]{0,6,5,4,3,2,1:T(8,128)(2,1)} copy(bf16[104,2,8,2,8,2,8]{6,5,4,3,2,1,0:T(2,128)(2,1)} %concatenate.102) | data formatting | bytes 1703936 | tf_op jit(solution)/shard_map/concatenate | solution.py:207
  470.1 20.5 %copy.183 = bf16[224,2,2,2,8,8,8]{6,5,4,3,2,1,0:T(8,128)(2,1)} copy(bf16[224,2,2,2,8,8,8]{0,6,3,5,2,4,1:T(8,128)(2,1)S(1)} %maximum_bitcast_fusion.1) | data formatting | bytes 3670016 | tf_op jit(solution)/shard_map/transpose | solution.py:121
  493.4 42.0 %reshape.803 = bf16[1792,512]{1,0:T(8,128)(2,1)S(1)} reshape(bf16[224,2,2,2,8,8,8]{6,5,4,3,2,1,0:T(8,128)(2,1)} %copy.183) | data formatting | bytes 3670016 | tf_op jit(solution)/shard_map/reshape | solution.py:121
  538.1 3.6 convolution_bitcast_fusion
  (310 shorter events, 182.7 us)
Async XLA Ops:
  2.5 28.3 %collective-permute-start.10 = (bf16[1,1,1,8,3]{3,4,2,1,0:T(4,128)(2,1)S(1)}, bf16[1,1,1,8,3]{3,4,2,1,0:T(4,128)(2,1)S(1)}, u32[]{:S(2)}, u32[]{:S(2)}) collective-permute-start(bf16[1,1,1,8,3]{3,4,2,1,0:T(4,128)(2,1)S(1)} %bitcast.248), channel_id=1, source_target_pairs={{8,0},{16,8},{24,16},{0,24},{9,1},{17,9},{25,17},{1,25},{10,2},{18... | collective-permute-start | bytes 152 | tf_op jit(solution)/shard_map/ppermute | solution.py:66
  6.4 24.4 %collective-permute-start.9 = (bf16[1,1,1,8,3]{3,4,2,1,0:T(4,128)(2,1)S(1)}, bf16[1,1,1,8,3]{3,4,2,1,0:T(4,128)(2,1)S(1)}, u32[]{:S(2)}, u32[]{:S(2)}) collective-permute-start(bf16[1,1,1,8,3]{3,4,2,1,0:T(4,128)(2,1)S(1)} %bitcast.249), channel_id=1, source_target_pairs={{0,8},{8,16},{16,24},{24,0},{1,9},{9,17},{17,25},{25,1},{2,10},{10... | collective-permute-start | bytes 152 | tf_op jit(solution)/shard_map/ppermute | solution.py:63
  8.5 52.5 %collective-permute-start.4 = (bf16[1,1,1,8,16,256]{5,4,3,2,1,0:T(8,128)(2,1)}, bf16[1,1,1,8,16,256]{5,4,3,2,1,0:T(8,128)(2,1)}, u32[]{:S(2)}, u32[]{:S(2)}) collective-permute-start(bf16[1,1,1,8,16,256]{5,4,3,2,1,0:T(8,128)(2,1)} %bitcast.15), channel_id=1, source_target_pairs={{8,0},{16,8},{24,16},{0,24},{9,1},{17,9},{25,17},{1,25},{10,2},{18... | collective-permute-start | bytes 196616 | tf_op jit(solution)/shard_map/ppermute | solution.py:66
  11.5 49.6 %collective-permute-start.3 = (bf16[1,1,1,8,16,256]{5,4,3,2,1,0:T(8,128)(2,1)}, bf16[1,1,1,8,16,256]{5,4,3,2,1,0:T(8,128)(2,1)}, u32[]{:S(2)}, u32[]{:S(2)}) collective-permute-start(bf16[1,1,1,8,16,256]{5,4,3,2,1,0:T(8,128)(2,1)} %bitcast.15), channel_id=1, source_target_pairs={{0,8},{8,16},{16,24},{24,0},{1,9},{9,17},{17,25},{25,1},{2,10},{10... | collective-permute-start | bytes 196616 | tf_op jit(solution)/shard_map/ppermute | solution.py:63
  12.9 32.4 %collective-permute-start = (bf16[8,40,40]{1,2,0:T(8,128)(2,1)S(1)}, bf16[8,40,40]{1,2,0:T(8,128)(2,1)S(1)}, u32[]{:S(2)}, u32[]{:S(2)}) collective-permute-start(bf16[8,40,40]{1,2,0:T(8,128)(2,1)S(1)} %slice.163), channel_id=1, source_target_pairs={{0,24},{8,0},{16,8},{24,16},{1,25},{9,1},{17,9},{25,17},{2,26},{10... | collective-permute-start | bytes 76808 | tf_op jit(solution)/shard_map/ppermute | solution.py:54
  22.7 132.4 %copy-start.2 = (bf16[1,1,1,16,16,256]{3,5,4,2,1,0:T(8,128)(2,1)}, bf16[1,1,1,16,16,256]{3,5,4,2,1,0:T(8,128)(2,1)S(1)}, u32[]{:S(2)}) copy-start(bf16[1,1,1,16,16,256]{3,5,4,2,1,0:T(8,128)(2,1)S(1)} %copy.148) | copy-start | bytes 393220
  30.9 5.0 collective-permute-start.12
  34.5 5.4 collective-permute-start.11
  39.9 3.8 collective-permute-start.14
  40.0 3.8 collective-permute-start.13
  46.2 13.5 %collective-permute-start.1 = (bf16[48,8,40]{1,2,0:T(8,128)(2,1)}, bf16[48,8,40]{1,2,0:T(8,128)(2,1)}, u32[]{:S(2)}, u32[]{:S(2)}) collective-permute-start(bf16[48,8,40]{1,2,0:T(8,128)(2,1)} %fusion.3), channel_id=1, source_target_pairs={{0,6},{2,0},{4,2},{6,4},{1,7},{3,1},{5,3},{7,5},{8,14},{10,8},{12,... | collective-permute-start | bytes 92168 | tf_op jit(solution)/shard_map/ppermute | solution.py:54
  60.9 3.9 collective-permute-start.2
  62.6 87.0 %collective-permute-start.6 = (bf16[3,1,1,8,16,256]{5,4,3,2,1,0:T(8,128)(2,1)}, bf16[3,1,1,8,16,256]{5,4,3,2,1,0:T(8,128)(2,1)}, u32[]{:S(2)}, u32[]{:S(2)}) collective-permute-start(bf16[3,1,1,8,16,256]{5,4,3,2,1,0:T(8,128)(2,1)} %pad_maximum_fusion.9), channel_id=1, source_target_pairs={{2,0},{4,2},{6,4},{0,6},{3,1},{5,3},{7,5},{1,7},{10,8},{12,10},{14... | collective-permute-start | bytes 589832 | tf_op jit(solution)/shard_map/ppermute | solution.py:66
  64.7 84.9 %collective-permute-start.5 = (bf16[3,1,1,8,16,256]{5,4,3,2,1,0:T(8,128)(2,1)}, bf16[3,1,1,8,16,256]{5,4,3,2,1,0:T(8,128)(2,1)}, u32[]{:S(2)}, u32[]{:S(2)}) collective-permute-start(bf16[3,1,1,8,16,256]{5,4,3,2,1,0:T(8,128)(2,1)} %pad_maximum_fusion.9), channel_id=1, source_target_pairs={{0,2},{2,4},{4,6},{6,0},{1,3},{3,5},{5,7},{7,1},{8,10},{10,12},{12... | collective-permute-start | bytes 589832 | tf_op jit(solution)/shard_map/ppermute | solution.py:63
  151.7 12.5 %collective-permute-start.8 = (bf16[3,3,1,8,16,256]{5,4,3,2,1,0:T(8,128)(2,1)}, bf16[3,3,1,8,16,256]{5,4,3,2,1,0:T(8,128)(2,1)}, u32[]{:S(2)}, u32[]{:S(2)}) collective-permute-start(bf16[3,3,1,8,16,256]{5,4,3,2,1,0:T(8,128)(2,1)} %pad_maximum_fusion.4), channel_id=1, source_target_pairs={{1,0},{0,1},{3,2},{2,3},{5,4},{4,5},{7,6},{6,7},{9,8},{8,9},{11,10... | collective-permute-start | bytes 1769480 | tf_op jit(solution)/shard_map/ppermute | solution.py:66
  151.9 12.2 %collective-permute-start.7 = (bf16[3,3,1,8,16,256]{5,4,3,2,1,0:T(8,128)(2,1)}, bf16[3,3,1,8,16,256]{5,4,3,2,1,0:T(8,128)(2,1)}, u32[]{:S(2)}, u32[]{:S(2)}) collective-permute-start(bf16[3,3,1,8,16,256]{5,4,3,2,1,0:T(8,128)(2,1)} %pad_maximum_fusion.4), channel_id=1, source_target_pairs={{0,1},{1,0},{2,3},{3,2},{4,5},{5,4},{6,7},{7,6},{8,9},{9,8},{10,11... | collective-permute-start | bytes 1769480 | tf_op jit(solution)/shard_map/ppermute | solution.py:63
  338.9 5.3 collective-permute-start.16
  339.0 5.6 %collective-permute-start.15 = (bf16[1,1,1,8,16,256]{5,4,3,2,1,0:T(8,128)(2,1)S(1)}, bf16[1,1,1,8,16,256]{5,4,3,2,1,0:T(8,128)(2,1)S(1)}, u32[]{:S(2)}, u32[]{:S(2)}) collective-permute-start(bf16[1,1,1,8,16,256]{5,4,3,2,1,0:T(8,128)(2,1)S(1)} %bitcast.241), channel_id=1, source_target_pairs={{0,8},{8,16},{16,24},{24,0},{1,9},{9,17},{17,25},{25,1},{2,10},{10... | collective-permute-start | bytes 196616 | tf_op jit(solution)/shard_map/ppermute | solution.py:63
  344.6 9.2 %collective-permute-start.18 = (bf16[3,1,1,8,16,256]{5,4,3,2,1,0:T(8,128)(2,1)S(1)}, bf16[3,1,1,8,16,256]{5,4,3,2,1,0:T(8,128)(2,1)S(1)}, u32[]{:S(2)}, u32[]{:S(2)}) collective-permute-start(bf16[3,1,1,8,16,256]{5,4,3,2,1,0:T(8,128)(2,1)S(1)} %pad_maximum_fusion.10), channel_id=1, source_target_pairs={{2,0},{4,2},{6,4},{0,6},{3,1},{5,3},{7,5},{1,7},{10,8},{12,10},{14... | collective-permute-start | bytes 589832 | tf_op jit(solution)/shard_map/ppermute | solution.py:66
  348.4 8.8 %collective-permute-start.17 = (bf16[3,1,1,8,16,256]{5,4,3,2,1,0:T(8,128)(2,1)S(1)}, bf16[3,1,1,8,16,256]{5,4,3,2,1,0:T(8,128)(2,1)S(1)}, u32[]{:S(2)}, u32[]{:S(2)}) collective-permute-start(bf16[3,1,1,8,16,256]{5,4,3,2,1,0:T(8,128)(2,1)S(1)} %pad_maximum_fusion.10), channel_id=1, source_target_pairs={{0,2},{2,4},{4,6},{6,0},{1,3},{3,5},{5,7},{7,1},{8,10},{10,12},{12... | collective-permute-start | bytes 589832 | tf_op jit(solution)/shard_map/ppermute | solution.py:63
  358.1 10.1 %collective-permute-start.20 = (bf16[3,3,1,8,16,256]{5,4,3,2,1,0:T(8,128)(2,1)}, bf16[3,3,1,8,16,256]{5,4,3,2,1,0:T(8,128)(2,1)}, u32[]{:S(2)}, u32[]{:S(2)}) collective-permute-start(bf16[3,3,1,8,16,256]{5,4,3,2,1,0:T(8,128)(2,1)} %pad_maximum_fusion.5), channel_id=1, source_target_pairs={{1,0},{0,1},{3,2},{2,3},{5,4},{4,5},{7,6},{6,7},{9,8},{8,9},{11,10... | collective-permute-start | bytes 1769480 | tf_op jit(solution)/shard_map/ppermute | solution.py:66
  358.1 10.1 %collective-permute-start.19 = (bf16[3,3,1,8,16,256]{5,4,3,2,1,0:T(8,128)(2,1)}, bf16[3,3,1,8,16,256]{5,4,3,2,1,0:T(8,128)(2,1)}, u32[]{:S(2)}, u32[]{:S(2)}) collective-permute-start(bf16[3,3,1,8,16,256]{5,4,3,2,1,0:T(8,128)(2,1)} %pad_maximum_fusion.5), channel_id=1, source_target_pairs={{0,1},{1,0},{2,3},{3,2},{4,5},{5,4},{6,7},{7,6},{8,9},{9,8},{10,11... | collective-permute-start | bytes 1769480 | tf_op jit(solution)/shard_map/ppermute | solution.py:63
  389.2 29.5 %copy-start.4 = (bf16[13,8,16,256]{3,2,1,0:T(8,128)(2,1)S(1)}, bf16[13,8,16,256]{3,2,1,0:T(8,128)(2,1)}, u32[]{:S(2)}) copy-start(bf16[13,8,16,256]{3,2,1,0:T(8,128)(2,1)} %get-tuple-element.37) | copy-start | bytes 2555908
  470.1 20.5 %copy-start.10 = (bf16[2,16,8,512,1]{3,2,4,1,0:T(8,128)(2,1)S(1)}, bf16[2,16,8,512,1]{3,2,4,1,0:T(8,128)(2,1)}, u32[]{:S(2)}) copy-start(bf16[2,16,8,512,1]{3,2,4,1,0:T(8,128)(2,1)} %copy.193) | copy-start | bytes 786436
  (30 other events, 185.2 us)
where the time goes:
time: 555 us; the launch traced here: 544 us
  local copies, waits for them, and re-layouts  448 us (81%)
  other arithmetic  28.7 us (5%)
  starting transfers between devices  23.2 us (4%)
  waiting for transfers between devices  22.9 us (4%)
  matrix products  19.9 us (4%)
    concatenate x8, local copies, waits for them, and re-layouts, local(): jnp.concatenate([current, picked_boxes[:13].reshape(-1, width, width * wi...  187 us
    reshape x2, local copies, waits for them, and re-layouts, octants(): split_up.transpose(0, 1, 3, 5, 2, 4, 6).reshape(amount * 8, half_width ** 3)  84.3 us
    gather x80, local copies, waits for them, and re-layouts  80.1 us
    transpose x6, local copies, waits for them, and re-layouts, octants(): split_up.transpose(0, 1, 3, 5, 2, 4, 6).reshape(amount * 8, half_width ** 3)  46.7 us
    ppermute x9, starting transfers between devices, padded(): lax.ppermute(lax.slice_in_dim(block, 0, width, axis=dim), axis, backward)  16.8 us
    dot_general x4, local copies, waits for them, and re-layouts, combine(): jnp.einsum('ak,bk->ab', stacked, columns, preferred_element_type=jnp.floa...  12.2 us
  transfers between devices with their start and end apart: 21, of which 6 were waited for; matrix products, arithmetic and copies ran while one was open for 26% of the time, Pallas kernels for 0%

commit v1 on v0

v1 whole, which is shorter than its diff:
```python
import functools

import jax
import jax.numpy as jnp
import ml_dtypes
import numpy as np
from jax import lax
from jax.experimental import pallas as pl
from jax.experimental.pallas import tpu as pltpu
from jax.sharding import PartitionSpec as P

REGION = 5
SWEEPS = 2
MAGIC = [
    8.433424733352934e-07,
    -1.290557201342061e-05,
    8.76298447621056e-05,
    -0.00030158038132690465,
    0.001747237136729939,
    -0.009420470302010804,
    0.023738214637249424,
    0.0612625895831208,
    0.9940415697834004,
    -0.06048952891969835,
    -0.021030251609303816,
    0.013372634148547948,
    -0.0034412814449349387,
    0.0004944322768868992,
    -5.185986881173433e-05,
    2.7273449291197967e-06,
]
KINETIC = [
    -3.55369228991319,
    2.2191465938911166,
    -0.6156141465570069,
    0.2371780582153806,
    -0.0822663999742123,
    0.0220702918848226,
    -0.004097656893426338,
    0.00045167920287502236,
    -2.3982285245075998e-05,
    2.0904234952920368e-06,
    -3.7230763047369276e-07,
    -1.0585705549674146e-08,
    -5.8138798302825403e-11,
    2.7080049362631943e-13,
    -6.9244749406392e-18,
]
CELL = 1.0 / 4096.0
STEP = 0.1
PENALTY = 3.0
BF = jnp.bfloat16
F32 = jnp.float32
MESH = pl.DeviceIdType.MESH
AXES = ("gx", "gy", "gz")

PCOL, PCOLT, PROW, RM, RK, RMT, LM, LMT, LK = 0, 1, 2, 3, 5, 7, 9, 11, 13


def make_tables():
    magic = np.zeros((16, 16))
    kinetic = np.zeros((16, 16))
    for r in range(16):
        for c in range(16):
            if -8 <= c - r <= 7:
                magic[r, c] = MAGIC[c - r + 8]
            if abs(c - r) <= 14:
                kinetic[r, c] = KINETIC[abs(c - r)]
    new = np.arange(256)
    py, pz, yy, zz = new // 128, new // 64 % 2, new // 8 % 8, new % 8
    old = (8 * py + yy) * 16 + 8 * pz + zz
    pcol = np.zeros((256, 256))
    pcol[old, new] = 1.0
    prow = np.zeros((256, 256))
    prow[new, (new % 16) * 16 + new // 16] = 1.0
    eye = np.eye(16)
    rm = np.kron(magic, magic).T[old][:, old]
    rk = -0.5 * (np.kron(kinetic, eye) + np.kron(eye, kinetic))[old][:, old]
    lm = np.kron(magic, eye)
    lk = -0.5 * np.kron(kinetic, eye)
    out = [pcol, pcol.T, prow]
    for table in (rm, rk, rm.T, lm, lm.T, lk):
        high = table.astype(np.float32).astype(ml_dtypes.bfloat16)
        out += [high, table - high.astype(np.float64)]
    return np.stack([np.asarray(t, np.float32).astype(ml_dtypes.bfloat16) for t in out])


def offsets(count):
    return (0, 1) if count == 2 else (-1, 0, 1)


def plan(counts):
    start, place, slot_of = 0, {}, []
    for dx in offsets(counts[0]):
        for dy in offsets(counts[1]):
            for dz in offsets(counts[2]):
                if (dx, dy, dz) == (0, 0, 0):
                    continue
                slabs = (1 if dx else 2) * (1 if dy else 2)
                place[(dx, dy, dz)] = start
                slot_of += [len(place)] * slabs
                start += slabs
    total = -(-start // 8) * 8
    slot_of += [0] * (total - start)
    messages = []
    for (dx, dy, dz), first in place.items():
        ex, ey = -dx, -dy
        ez = dz if counts[2] == 2 else -dz
        px, py = (0 if ex < 0 else 1), (0 if ey < 0 else 1)
        if ex and ey:
            messages.append(((ex, ey, ez), (px, pl.ds(py, 1)), first, 1))
        elif ex:
            messages.append(((ex, ey, ez), (px,), first, 2))
        elif ey:
            messages.append(((ex, ey, ez), (slice(None), py), first, 2))
        else:
            messages.append(((ex, ey, ez), (0,), first, 2))
            messages.append(((ex, ey, ez), (1,), first + 2, 2))
    return messages, start, total, slot_of


def mm(a, b):
    return jnp.dot(a, b, preferred_element_type=F32)


def mm_nt(a, b):
    return lax.dot_general(a, b, (((1,), (1,)), ((), ())), preferred_element_type=F32)


def iota(shape, dim):
    return lax.broadcasted_iota(jnp.int32, shape, dim)


def to_octants(value):
    rows = []
    for px in range(2):
        for block in range(4):
            rows.append(
                jnp.concatenate(
                    [
                        value[px * 128 + x * 16 : px * 128 + x * 16 + 16, block * 64 : block * 64 + 64]
                        for x in range(8)
                    ],
                    axis=1,
                )
            )
    return jnp.concatenate(rows, axis=0)


def from_octants(value):
    rows = []
    for px in range(2):
        for x in range(8):
            rows.append(
                jnp.concatenate(
                    [
                        value[(px * 4 + block) * 16 : (px * 4 + block) * 16 + 16, x * 64 : x * 64 + 64]
                        for block in range(4)
                    ],
                    axis=1,
                )
            )
    return jnp.concatenate(rows, axis=0)


def kernel(
    counts, messages, used, slabs,
    box_ref, anchor_ref, pot_ref, tables_hbm, same_hbm,
    out_ref,
    tab, same, ex1, ex2, recv1, recv2,
    halo, hx, hy, hz, hxy, hxz, hyz, hxyz,
    tab_sem, send_sem, recv_sem, halo_send, halo_recv,
):
    me = [lax.axis_index(name) for name in AXES]

    def device(offset):
        return tuple(
            lax.rem(me[i] + (offset[i] + counts[i]), counts[i]) if offset[i] else me[i]
            for i in range(3)
        )

    tab_copy = pltpu.make_async_copy(tables_hbm, tab, tab_sem.at[0])
    same_copy = pltpu.make_async_copy(same_hbm, same, tab_sem.at[1])
    tab_copy.start()
    same_copy.start()

    targets = sorted({m[0] for m in messages})
    barrier = pltpu.get_barrier_semaphore()
    for offset in targets:
        pl.semaphore_signal(barrier, inc=1, device_id=device(offset), device_id_type=MESH)

    z = iota((40, 384), 0)
    lane = iota((40, 384), 1)
    base = lane - ((z // 8) * 64 + z % 8)
    own = None
    for y in range(8):
        picked = jnp.concatenate(
            [pot_ref[pl.ds(by * 8 + y, 40, stride=40), :] for by in range(5)], axis=0
        ).astype(BF)
        part = mm(picked, (base == 8 * y).astype(F32).astype(BF))
        own = part if own is None else own + part
    for by in range(5):
        halo[by] = jnp.concatenate(
            [own[by * 40 : by * 40 + 40], jnp.zeros((8, 384), F32)], axis=0
        ).astype(BF)

    anchor = anchor_ref[...]
    coord = [anchor[:, i : i + 1] for i in range(3)]
    touch = functools.reduce(
        jnp.maximum,
        [((c == 0) | (c == REGION - 1)).astype(F32) for c in coord],
    )
    row_f = iota((16, 128), 0)
    lane_f = iota((16, 128), 1) % 16
    rank = jnp.sum(jnp.where(row_f < lane_f, touch, 0.0), axis=0, keepdims=True)
    touched = jnp.sum(jnp.where(row_f == lane_f, touch, 0.0), axis=0, keepdims=True)
    row_s = iota((64, 128), 0)
    lane_s = iota((64, 128), 1)
    select = jnp.where(
        (row_s // 8 == lane_s // 16) & ((row_s % 8).astype(F32) == rank) & (touched > 0.5), 1.0, 0.0
    ).astype(BF)
    lanes = iota((16, 128), 1)
    hots = []
    for p in range(8):
        hot, first = None, 0
        for i, bit in enumerate((p // 4, p // 2 % 2, p % 2)):
            span = REGION * counts[i]
            value = coord[i] + (me[i] * REGION + bit)
            value = jnp.where(value >= span, value - span, value) + first
            part = (lanes == value).astype(F32)
            hot = part if hot is None else hot + part
            first += span
        hots.append(hot)
    hot = jnp.concatenate(hots, axis=0).astype(BF)

    tab_copy.wait()
    permuted = mm(box_ref[...], tab[PCOL]).astype(BF)
    current_f = mm(tab[PROW], permuted)

    recv1[used:] = jnp.zeros((slabs - used, 16, 640), BF)
    recv2[used:] = jnp.zeros((slabs - used, 16, 512), BF)
    pl.semaphore_wait(barrier, len(targets))

    def halo_copy(n, src, dst, offset):
        return pltpu.make_async_remote_copy(
            src_ref=src, dst_ref=dst, send_sem=halo_send.at[n], recv_sem=halo_recv.at[n],
            device_id=device(offset), device_id_type=MESH,
        )

    low = 1 if counts[2] == 2 else -1
    halos = [
        halo_copy(0, halo.at[:, pl.ds(0, 16), :], hx, (-1, 0, 0)),
        halo_copy(1, halo.at[pl.ds(0, 1)], hy, (0, -1, 0)),
        halo_copy(2, halo.at[:, :, pl.ds(0, 128)], hz, (0, 0, low)),
        halo_copy(3, halo.at[pl.ds(0, 1), pl.ds(0, 16), :], hxy, (-1, -1, 0)),
        halo_copy(4, halo.at[:, pl.ds(0, 16), pl.ds(0, 128)], hxz, (-1, 0, low)),
        halo_copy(5, halo.at[pl.ds(0, 1), :, pl.ds(0, 128)], hyz, (0, -1, low)),
        halo_copy(6, halo.at[pl.ds(0, 1), pl.ds(0, 16), pl.ds(0, 128)], hxyz, (-1, -1, low)),
    ]
    for copy in halos:
        copy.start()

    def exchange(sweep, source, target):
        copies = []
        for n, (offset, index, first, count) in enumerate(messages):
            copies.append(
                pltpu.make_async_remote_copy(
                    src_ref=source.at[index],
                    dst_ref=target.at[pl.ds(first, count)],
                    send_sem=send_sem.at[sweep, n],
                    recv_sem=recv_sem.at[sweep, n],
                    device_id=device(offset),
                    device_id_type=MESH,
                )
            )
        for copy in copies:
            copy.start()
        return copies

    def double(a, b):
        return mm(a, tab[b]) + mm(a, tab[b + 1])

    def double_left(a, b):
        return mm(tab[a], b) + mm(tab[a + 1], b)

    potential = None
    mask_own = mm_nt(hot, hot) > 2.5
    col_o = iota((128, 128), 1) % 16
    same_own = (iota((128, 128), 0) % 16 == col_o).astype(F32).astype(BF)
    delta = jnp.where(iota((16, 128), 0) == iota((16, 128), 1) % 16, PENALTY, 0.0)
    mask_recv = None
    all_copies = list(halos)

    def weights(overlap, mask, table, extra):
        width = overlap.shape[1]
        kept = jnp.where(mask, overlap, 0.0).reshape(8, 16, width).sum(axis=0)
        high = kept.astype(BF)
        rest = (kept - high.astype(F32)).astype(BF)
        coupling = (mm(high, table) + mm(rest, table)) * CELL
        if extra is not None:
            coupling = coupling + extra
        spread = jnp.concatenate([coupling] * 8, axis=0)
        return jnp.where(mask, spread, 0.0).astype(BF)

    for sweep in range(SWEEPS):
        current = current_f.astype(BF)
        octs = to_octants(current_f).astype(BF)
        if sweep == 0:
            ex1[...] = mm(select, jnp.concatenate([octs, hot], axis=1)).astype(BF).reshape(2, 2, 16, 640)
            copies = exchange(0, ex1, recv1)
        else:
            ex2[...] = mm(select, octs).astype(BF).reshape(2, 2, 16, 512)
            copies = exchange(1, ex2, recv2)
        all_copies += copies

        on_grid = double_left(LM, double(current, RM).astype(BF))
        kinetic = double(current, RK) + double_left(LK, current)

        if sweep == 0:
            for copy in halos:
                copy.wait_recv()
            pieces = []
            for by in range(6):
                if by < 5:
                    parts = (halo[by], hx[by], hz[by], hxz[by])
                else:
                    parts = (hy[0], hxy[0], hyz[0], hxyz[0])
                a, b, c, d = [part.astype(F32) for part in parts]
                body = jnp.concatenate([a[:40], b[:8]], axis=0)
                side = jnp.concatenate([c[:40], d[:8]], axis=0)
                pieces.append(
                    jnp.concatenate(
                        [body[:, :256], jnp.concatenate([body[:, 256:320], side[:, :64]], axis=1)], axis=1
                    )
                )
            pieces.append(jnp.zeros((96, 384), F32))
            extended = jnp.concatenate(pieces, axis=0).astype(BF)
            column = iota((16, 384), 1)
            blocks = []
            depth = jnp.concatenate([coord[2]] * 16, axis=0)
            for py in range(2):
                start = (coord[1] + py) * 48 + coord[0] * 8
                rows = jnp.concatenate(
                    [(column == start + x).astype(F32) for x in range(16)], axis=0
                ).astype(BF)
                taken = mm(rows, extended)
                for pz in range(2):
                    block = jnp.zeros((256, 64), F32)
                    for bz in range(5):
                        at = (bz + pz) * 64
                        block = jnp.where(depth == bz, taken[:, at : at + 64], block)
                    blocks.append(block)
            potential = jnp.concatenate(blocks, axis=1)

        weighted = (potential * on_grid).astype(BF)
        applied = double_left(LMT, double(weighted, RMT).astype(BF)) + kinetic
        mixed = to_octants(applied - PENALTY * current_f).astype(BF)
        w_own = weights(mm_nt(mixed, octs), mask_own, same_own, delta)
        correction = mm(w_own, octs)

        if sweep == 0:
            same_copy.wait()
        for copy in copies:
            copy.wait_recv()
        if sweep == 0:
            received = recv1[...].reshape(slabs * 16, 640)
            mask_recv = mm_nt(hot, received[:, 512:]) > 2.5
            cands = received[:, :512]
        else:
            cands = recv2[...].reshape(slabs * 16, 512)
        w_recv = weights(mm_nt(mixed, cands), mask_recv, same[...], None)
        correction = from_octants(correction + mm(w_recv, cands))
        current_f = (current_f - STEP * (applied - correction)).astype(BF).astype(F32)

    back = mm(tab[PROW], current_f.astype(BF)).astype(BF)
    out_ref[...] = mm(back, tab[PCOLT]).astype(BF)
    for copy in all_copies:
        copy.wait_send()


def solution(mesh):
    counts = tuple(mesh.shape[name] for name in AXES)
    messages, used, slabs, slot_of = plan(counts)
    slot = np.repeat(np.array(slot_of), 16)
    item = np.arange(slabs * 16) % 8
    same = (slot[:, None] == slot[None, :]) & (item[:, None] == item[None, :])
    same = same.astype(np.float32).astype(ml_dtypes.bfloat16)
    tables = make_tables()
    vmem = pl.BlockSpec(memory_space=pltpu.VMEM)
    anyspace = pl.BlockSpec(memory_space=pl.ANY)

    def local(boxes, anchors, potential):
        shape = boxes.shape
        out = pl.pallas_call(
            functools.partial(kernel, counts, messages, used, slabs),
            out_shape=jax.ShapeDtypeStruct((256, 256), BF),
            in_specs=[vmem, vmem, vmem, anyspace, anyspace],
            out_specs=vmem,
            scratch_shapes=[
                pltpu.VMEM(tables.shape, BF),
                pltpu.VMEM(same.shape, BF),
                pltpu.VMEM((2, 2, 16, 640), BF),
                pltpu.VMEM((2, 2, 16, 512), BF),
                pltpu.VMEM((slabs, 16, 640), BF),
                pltpu.VMEM((slabs, 16, 512), BF),
                pltpu.VMEM((5, 48, 384), BF),
                pltpu.VMEM((5, 16, 384), BF),
                pltpu.VMEM((1, 48, 384), BF),
                pltpu.VMEM((5, 48, 128), BF),
                pltpu.VMEM((1, 16, 384), BF),
                pltpu.VMEM((5, 16, 128), BF),
                pltpu.VMEM((1, 48, 128), BF),
                pltpu.VMEM((1, 16, 128), BF),
                pltpu.SemaphoreType.DMA((2,)),
                pltpu.SemaphoreType.DMA((SWEEPS, len(messages))),
                pltpu.SemaphoreType.DMA((SWEEPS, len(messages))),
                pltpu.SemaphoreType.DMA((7,)),
                pltpu.SemaphoreType.DMA((7,)),
            ],
            compiler_params=pltpu.CompilerParams(
                collective_id=0, has_side_effects=True, vmem_limit_bytes=40 * 1024 * 1024
            ),
        )(
            boxes.reshape(256, 256),
            anchors.reshape(16, 3),
            potential.reshape(1600, 40),
            jnp.asarray(tables),
            jnp.asarray(same),
        )
        return out.reshape(shape)

    placed = (
        P("gx", "gy", "gz", None, None, None),
        P("gx", "gy", "gz", None, None),
        P("gx", "gy", "gz"),
    )
    return jax.shard_map(
        local,
        mesh=mesh,
        in_specs=placed,
        out_specs=P("gx", "gy", "gz", None, None, None),
        check_vma=False,
    )
```

time: 555 us -> 37 us (0.07); the launches traced: 544 us -> 36.7 us
  local copies, waits for them, and re-layouts: 448 us -> 6.05 us
  Pallas kernels: 0 us -> 30.6 us
  other arithmetic: 28.7 us -> 0 us
  starting transfers between devices: 23.2 us -> 0 us
  waiting for transfers between devices: 22.9 us -> 0 us
  matrix products: 19.9 us -> 0 us
    concatenate x9 -> x0, local copies, waits for them, and re-layouts: 187 us -> none  [the longest x8 187 us: local(): jnp.concatenate([current, picked_boxes[:13].reshape(-1, width, width * wi...]
    reshape x7 -> x1, local copies, waits for them, and re-layouts: 88.9 us -> 0.76 us  [local(): anchors.reshape(16, 3)]
    gather x87 -> x0, local copies, waits for them, and re-layouts: 87.3 us -> none
    transpose x8 -> x0, local copies, waits for them, and re-layouts: 47.1 us -> none  [the longest x6 46.7 us: octants(): split_up.transpose(0, 1, 3, 5, 2, 4, 6).reshape(amount * 8, half_width ** 3)]
    pallas_call x0 -> x1, Pallas kernels: none -> 30.6 us  [local(): pl.pallas_call(functools.partial(kernel, counts, messages, used, slabs),...]
    ppermute x21 -> x0, starting transfers between devices: 23.2 us -> none  [the longest x9 16.8 us: padded(): lax.ppermute(lax.slice_in_dim(block, 0, width, axis=dim), axis, backward)]
    ppermute x21 -> x0, waiting for transfers between devices: 22.9 us -> none  [the longest x3 8.62 us: passed_along(): return lax.ppermute(value, axis, pairs)]
    dot_general x16 -> x0, matrix products: 19.9 us -> none  [the longest x2 7.27 us: combine(): correction = jnp.dot(weights, columns, preferred_element_type=jnp.float32)]
  transfers between devices with their start and end apart: 21 -> 0, of which waited for: 6 -> 0; matrix products, arithmetic and copies ran while one was open for 26% -> 0% of each run, Pallas kernels for 0% -> 0%
where the time goes in v1:
time: 37 us; the launch traced here: 36.7 us
  Pallas kernels  30.6 us (83%)
  local copies, waits for them, and re-layouts  6.05 us (16%)
    pallas_call x1, Pallas kernels, local(): pl.pallas_call(functools.partial(kernel, counts, messages, used, slabs),...  30.6 us
    unnamed x9, local copies, waits for them, and re-layouts  5.29 us
    reshape x1, local copies, waits for them, and re-layouts, local(): anchors.reshape(16, 3)  0.76 us

profile of v1, /device:TPU:0, one launch (start us, length us, event | category | flops | bytes accessed | tf_op | source)
XLA Modules:
  0.0 36.7 jit_solution(15124436115735841727)
XLA Ops:
  0.0 0.8 %copy.7 = s32[1,1,1,16,3]{4,3,2,1,0:T(8,128)S(1)} copy(s32[1,1,1,16,3]{3,2,4,1,0:T(1,128)} %param.6) | data formatting | bytes 384 | tf_op jit(solution)/shard_map/reshape | solution.py:425
  0.8 0.0 copy-start
  0.8 1.5 %copy-done = bf16[15,256,256]{2,1,0:T(8,128)(2,1)S(1)} copy-done((bf16[15,256,256]{2,1,0:T(8,128)(2,1)S(1)}, bf16[15,256,256]{2,1,0:T(8,128)(2,1)}, u32[]{:S(2)}) %copy-start) | copy-done | bytes 1966104
  2.3 0.0 copy-start.1
  2.3 1.1 %copy-done.1 = f32[40,40,40]{2,1,0:T(8,128)S(1)} copy-done((f32[40,40,40]{2,1,0:T(8,128)S(1)}, f32[40,40,40]{2,1,0:T(8,128)}, u32[]{:S(2)}) %copy-start.1) | copy-done | bytes 256024
  3.4 0.0 copy-start.2
  3.5 1.0 %copy-done.2 = bf16[512,512]{1,0:T(8,128)(2,1)S(1)} copy-done((bf16[512,512]{1,0:T(8,128)(2,1)S(1)}, bf16[512,512]{1,0:T(8,128)(2,1)}, u32[]{:S(2)}) %copy-start.2) | copy-done | bytes 524312
  4.5 0.0 copy-start.3
  4.5 0.9 %copy-done.3 = bf16[1,1,1,16,16,256]{5,4,3,2,1,0:T(8,128)(2,1)S(1)} copy-done((bf16[1,1,1,16,16,256]{5,4,3,2,1,0:T(8,128)(2,1)S(1)}, bf16[1,1,1,16,16,256]{5,4,3,2,1,0:T(8,128)(2,1)}, u32[]{:S(2)}) %copy-start.3) | copy-done | bytes 131096
  5.4 30.6 %shard_map.55 = bf16[256,256]{1,0:T(8,128)(2,1)S(1)} custom-call(bf16[256,256]{1,0:T(8,128)(2,1)S(1)} %bitcast.6, s32[16,3]{1,0:T(8,128)S(1)} %bitcast.7, f32[1600,40]{1,0:T(8,128)S(1)} %bitcast.4, bf16[15,256,256]{2,1,0:T(8,128)(2,1)S(1)} %copy-done, bf16[512,512]{1,0:T(8,128)(2,1)S(1)} %copy-done.2), custom_call_target="tpu_custom_call" | custom-call | tf_op jit(solution)/shard_map/pallas_call | solution.py:394
  36.0 0.7 %copy.9 = bf16[1,1,1,16,16,256]{5,4,3,2,1,0:T(8,128)(2,1)} copy(bf16[1,1,1,16,16,256]{5,4,3,2,1,0:T(8,128)(2,1)S(1)} %bitcast.5) | data formatting | bytes 262144
Async XLA Ops:
  0.8 1.5 %copy-start = (bf16[15,256,256]{2,1,0:T(8,128)(2,1)S(1)}, bf16[15,256,256]{2,1,0:T(8,128)(2,1)}, u32[]{:S(2)}) copy-start(bf16[15,256,256]{2,1,0:T(8,128)(2,1)} %constant.4.clone.tables_hbm) | copy-start | bytes 5898244
  2.3 1.1 %copy-start.1 = (f32[40,40,40]{2,1,0:T(8,128)S(1)}, f32[40,40,40]{2,1,0:T(8,128)}, u32[]{:S(2)}) copy-start(f32[40,40,40]{2,1,0:T(8,128)} %param.7) | copy-start | bytes 768004
  3.4 1.0 %copy-start.2 = (bf16[512,512]{1,0:T(8,128)(2,1)S(1)}, bf16[512,512]{1,0:T(8,128)(2,1)}, u32[]{:S(2)}) copy-start(bf16[512,512]{1,0:T(8,128)(2,1)} %constant.5.clone.same_hbm) | copy-start | bytes 1572868
  4.5 0.9 %copy-start.3 = (bf16[1,1,1,16,16,256]{5,4,3,2,1,0:T(8,128)(2,1)S(1)}, bf16[1,1,1,16,16,256]{5,4,3,2,1,0:T(8,128)(2,1)}, u32[]{:S(2)}) copy-start(bf16[1,1,1,16,16,256]{5,4,3,2,1,0:T(8,128)(2,1)} %param.5) | copy-start | bytes 393220
